TPU v7x, 32 devices: a whole 2x2x4 slice. The times are simulated.
32 devices in a mesh: gx: 8 (over y, x, core), gz: 4 (over z).
Axes of the slice: x: 2, y: 2, z: 4, core: 2. Of those that a mesh axis runs over, the one named last changes fastest.
Arguments:
- velocity: float32 [64, 3, 32, 32, 256], P(None, None, 'gx', 'gz'), may hold values from -40 to 40
- scaled_modes: float32 [64, 32, 32, 256], P(None, 'gx', 'gz'), may hold values from -70 to 70
Outputs:
- orthonormal: float32 [128, 32, 32, 256], P(None, 'gx', 'gz')
- triangle: float32 [128, 128], replicated
- lower_one: float32 [128, 128], replicated
All inputs are finite; a program needn't handle non-finite values.
Results may differ from a plain program's by a relative error of at most 0.0003.
Values sent between devices are 32-bit elements; how exact they have to be, the bound alone decides.
A program may use at most 128 MiB of HBM per device.

v0:
```python
import jax
import jax.numpy as jnp
from jax import lax
from jax.sharding import PartitionSpec as P

precise = lax.Precision.HIGHEST


def with_halo(block, sides, width):
    for axis, dim in sides:
        count = lax.axis_size(axis)
        forward = [(i, i + 1) for i in range(count - 1)]
        forward.append((count - 1, 0))
        backward = [(target, source) for source, target in forward]
        low = lax.ppermute(
            lax.slice_in_dim(block, block.shape[dim] - width, None, axis=dim), axis, forward
        )
        high = lax.ppermute(lax.slice_in_dim(block, 0, width, axis=dim), axis, backward)
        block = jnp.concatenate([low, block, high], axis=dim)
    return block


def along_wall(field):
    inner = (field[..., 2:] - field[..., :-2]) * 0.5
    bottom = (-3.0 * field[..., 0:1] + 4.0 * field[..., 1:2] - field[..., 2:3]) * 0.5
    top_side = (3.0 * field[..., -1:] - 4.0 * field[..., -2:-1] + field[..., -3:-2]) * 0.5
    return jnp.concatenate([bottom, inner, top_side], -1)


def product(left, right):
    return lax.dot_general(left, right, (((1,), (1,)), ((), ())), precision=precise)


def shards(velocity, scaled_modes):
    snapshots, _, cells_x, cells_z, cells_y = velocity.shape
    columns_old = scaled_modes.shape[0]
    total_cells = cells_x * lax.axis_size("gx") * cells_z * lax.axis_size("gz") * cells_y
    mode_fields = scaled_modes.reshape(columns_old, -1)
    mode_block = lax.psum(product(mode_fields, mode_fields), ("gx", "gz"))
    padded = with_halo(velocity, (("gx", 2), ("gz", 3)), 1)
    grad_x = (padded[:, :, 2:, 1:-1] - padded[:, :, :-2, 1:-1]) * 0.5
    grad_z = (padded[:, :, 1:-1, 2:] - padded[:, :, 1:-1, :-2]) * 0.5
    grad_y = along_wall(velocity)
    diagonal_part = (
        grad_x[:, 0] * grad_x[:, 0] + grad_z[:, 1] * grad_z[:, 1] + grad_y[:, 2] * grad_y[:, 2]
    )
    cross_part = (
        grad_z[:, 0] * grad_x[:, 1] + grad_y[:, 0] * grad_x[:, 2] + grad_y[:, 1] * grad_z[:, 2]
    )
    new_fields = (-0.5 * diagonal_part - cross_part).reshape(snapshots, -1)
    stacked = jnp.concatenate([mode_fields, new_fields], 0)
    cross_block, new_block = lax.psum(
        (product(mode_fields, new_fields), product(new_fields, new_fields)), ("gx", "gz")
    )
    upper_rows = jnp.concatenate([mode_block, cross_block], 1)
    lower_rows = jnp.concatenate([cross_block.T, new_block], 1)
    gram_sum = jnp.concatenate([upper_rows, lower_rows], 0)
    lower_one = jnp.linalg.cholesky(gram_sum / total_cells)
    first_pass = lax.linalg.triangular_solve(lower_one, stacked, left_side=True, lower=True)
    second_sum = lax.psum(product(first_pass, first_pass), ("gx", "gz"))
    lower_two = jnp.linalg.cholesky(second_sum / total_cells)
    basis = lax.linalg.triangular_solve(lower_two, first_pass, left_side=True, lower=True)
    triangle = jnp.dot(lower_two.T, lower_one.T, precision=precise)
    return (basis.reshape(stacked.shape[0], cells_x, cells_z, cells_y), triangle, lower_one)


def solution(mesh):
    in_specs = (P(None, None, "gx", "gz", None), P(None, "gx", "gz", None))
    out_specs = (P(None, "gx", "gz", None), P(), P())
    return jax.shard_map(shards, mesh=mesh, in_specs=in_specs, out_specs=out_specs, check_vma=False)
```

profile of v0, /device:TPU:0, one launch (start us, length us, event | category | flops | bytes accessed | tf_op | source)
XLA Modules:
  0.0 376.0 jit_solution(2215230563659253797)
XLA Ops:
  7.2 6.4 %copy.65 = f32[64,3,4,8,256]{4,0,3,2,1:T(8,128)S(1)} copy(f32[64,3,4,8,256]{4,3,2,1,0:T(8,128)} %param.5) | data formatting | bytes 12582912 | tf_op args[0]
  13.7 2.0 fusion.55
  15.6 2.7 copy-done.1
  18.8 3.0 collective-permute-start
  21.8 7.7 %fusion.54 = (f32[64,3,4,8,1]{4,3,2,1,0:T(8,128)}, f32[64,3,4,8,1]{4,3,2,1,0:T(8,128)}, f32[64,3,4,8,1]{4,3,2,1,0:T(8,128)}, f32[64,3,4,8,1]{4,3,2,1,0:T(8,128)}...) fusion(f32[64,3,4,8,256]{4,3,2,1,0:T(8,128)S(1)} %copy-done), kind=kLoop, calls=%fused_computation.72 | loop fusion | bytes 294912 | tf_op jit(solution)/shard_map/slice | solution.py:25
  29.5 2.7 copy.93
  32.2 2.7 copy.94
  34.9 2.7 copy.95
  37.5 2.7 copy.96
  40.2 2.7 copy.97
  42.9 1.4 copy.98
  44.3 9.8 %collective-permute-done.1 = f32[64,3,1,8,256]{4,0,3,2,1:T(8,128)} collective-permute-done((f32[64,3,1,8,256]{4,0,3,2,1:T(8,128)}, f32[64,3,1,8,256]{4,0,3,2,1:T(8,128)}, u32[]{:S(2)}, u32[]{:S(2)}) %collective-permute-start.1) | collective-permute-done | bytes 1572896 | tf_op jit(solution)/shard_map/ppermute | solution.py:15
  54.1 1.6 constant_dynamic-update-slice_fusion.2
  55.7 6.8 %constant_dynamic-update-slice_fusion.1 = f32[64,3,6,8,256]{4,0,3,2,1:T(8,128)S(1)} fusion(f32[64,3,6,8,256]{4,0,3,2,1:T(8,128)S(1)} %constant_dynamic-update-slice_fusion.2, f32[64,3,4,8,256]{4,3,2,1,0:T(8,128)} %param.5), kind=kLoop, calls=%fused_computation.64 | loop fusion | bytes 12582912
  62.5 1.6 constant_dynamic-update-slice_fusion
  64.1 3.6 copy-done.3
  67.7 1.6 fusion.53
  69.4 5.1 %collective-permute-start.2 = (f32[64,3,6,1,256]{4,0,3,2,1:T(8,128)}, f32[64,3,6,1,256]{4,0,3,2,1:T(8,128)}, u32[]{:S(2)}, u32[]{:S(2)}) collective-permute-start(f32[64,3,6,1,256]{4,0,3,2,1:T(8,128)} %get-tuple-element.10), channel_id=1, source_target_pairs={{1,0},{2,1},{3,2},{0,3},{5,4},{6,5},{7,6},{4,7},{9,8},{10,9},{11,1... | collective-permute-start | bytes 3538952 | tf_op jit(solution)/shard_map/ppermute | solution.py:18
  74.7 4.1 %fusion.22 = f32[64,64]{1,0:T(8,128)S(1)} fusion(f32[64,4,8,256]{3,2,1,0:T(8,128)S(1)} %copy-done.4), kind=kOutput, calls=%fused_computation.34 | convolution fusion | flops 402653184 | bytes 2113536 | tf_op jit(solution)/shard_map/dot_general | solution.py:31
  78.8 2.3 copy.77
  81.1 2.2 copy.78
  83.3 2.6 copy.99
  85.9 9.1 %fusion = f32[64,3,4,8,254]{4,0,3,2,1:T(8,128)} fusion(f32[64,3,4,8,256]{4,0,3,2,1:T(8,128)} %copy-done.1), kind=kLoop, calls=%fused_computation.1 | loop fusion | flops 3121152 | bytes 18726912 | tf_op jit(solution)/shard_map/mul | solution.py:24
  95.0 7.3 %pad_maximum_fusion.4 = f32[64,3,4,8,256]{4,0,3,2,1:T(8,128)S(1)} fusion(f32[64,3,4,8,1]{4,0,3,2,1:T(8,128)} %copy.78, f32[64,3,4,8,254]{4,0,3,2,1:T(8,128)} %fusion, f32[64,3,4,8,1]{4,0,3,2,1:T(8,128)} %copy.77), kind=kLoop, calls=%fused_computation.10 | loop fusion | flops 3145728 | bytes 12582912 | tf_op jit(solution)/shard_map/concatenate | solution.py:27
  102.3 2.6 fusion.4
  105.0 19.7 %collective-permute-done.3 = f32[64,3,6,1,256]{4,0,3,2,1:T(8,128)} collective-permute-done((f32[64,3,6,1,256]{4,0,3,2,1:T(8,128)}, f32[64,3,6,1,256]{4,0,3,2,1:T(8,128)}, u32[]{:S(2)}, u32[]{:S(2)}) %collective-permute-start.3) | collective-permute-done | bytes 1179680 | tf_op jit(solution)/shard_map/ppermute | solution.py:15
  124.7 5.4 %fusion.2 = f32[64,3,4,8,256]{4,0,3,2,1:T(8,128)S(1)} fusion(f32[64,3,6,8,256]{4,0,3,2,1:T(8,128)} %copy-done.3, f32[64,3,6,1,256]{4,0,3,2,1:T(8,128)} %collective-permute-done.3, f32[64,3,6,1,256]{4,0,3,2,1:T(8,128)} %collective-permute-done.2), kind=kLoop, calls=%fused_computation.4 | loop fusion | flops 6291456 | bytes 18087936 | tf_op jit(solution)/shard_map/mul | solution.py:42
  130.1 2.4 fusion.10
  132.6 2.8 fusion.25
  135.4 1.8 fusion.30
  137.2 1.2 copy.84
  138.4 41.1 %all-reduce = (f32[64,64]{0,1:T(8,128)S(1)}, f32[64,64]{1,0:T(8,128)S(1)}, f32[64,64]{1,0:T(8,128)S(1)}) all-reduce(f32[64,64]{0,1:T(8,128)S(1)} %fusion.30, f32[64,64]{1,0:T(8,128)S(1)} %fusion.25, f32[64,64]{1,0:T(8,128)S(1)} %fusion.22), channel_id=1, replica_groups=mesh['gx'=8,'gz'=4] {'gx','gz'}, use_global_device_ids=true, to_apply=%region_2.0 | all-reduce | flops 12288 | bytes 98304 | tf_op jit(solution)/shard_map/psum | solution.py:52
  180.0 11.7 %cholesky.44 = f32[128,128]{1,0:T(8,128)S(1)} custom-call(f32[128,128]{1,0:T(8,128)S(1)} %fusion.37), custom_call_target="Cholesky" | custom-call | tf_op jit(solution)/shard_map/jit(cholesky)/cholesky | solution.py:58
  191.7 0.6 compare_reduce_fusion.1
  192.4 0.7 fusion.41
  193.1 9.8 %custom-call.6 = f32[1,128,128]{1,2,0:T(8,128)S(1)} custom-call(f32[1,128,128]{2,1,0:T(8,128)S(1)} %get-tuple-element.8), custom_call_target="InvertDiagBlocksLowerTriangular" | custom-call | tf_op jit(solution)/shard_map/triangular_solve/custom-call.0 | solution.py:59
  202.9 1.5 reshape.64
  204.4 5.6 %fusion.5 = f32[128,8192]{1,0:T(8,128)S(1)} fusion(f32[64,8192]{1,0:T(8,128)} %reshape.64, f32[64,8192]{1,0:T(8,128)} %bitcast.56, f32[1,128,128]{1,2,0:T(8,128)S(1)} %custom-call.6), kind=kOutput, calls=%fused_computation.11 | convolution fusion | flops 1611661312 | bytes 8454144 | tf_op jit(solution)/shard_map/triangular_solve/dot.1 | solution.py:59
  210.0 2.0 copy-done.2
  212.0 4.0 %fusion.56 = f32[128,128]{0,1:T(8,128)} fusion(f32[128,8192]{1,0:T(8,128)S(1)} %fusion.5), kind=kOutput, calls=%fused_computation.74 | convolution fusion | flops 1610612736 | bytes 4259840 | tf_op jit(solution)/shard_map/dot_general | solution.py:31
  216.1 118.0 %all-reduce.3.cloned.1.call-done = f32[128,128]{0,1:T(8,128)} async-done(((f32[128,128]{0,1:T(8,128)}), f32[128,128]{0,1:T(8,128)}) %all-reduce.3.cloned.1.call-update) | async-done | bytes 65552 | tf_op jit(solution)/shard_map/psum | solution.py:60
  334.1 0.8 broadcast_multiply_fusion
  335.0 0.9 fusion.35
  335.9 11.7 %cholesky.55 = f32[128,128]{1,0:T(8,128)S(1)} custom-call(f32[128,128]{1,0:T(8,128)S(1)} %fusion.35), custom_call_target="Cholesky" | custom-call | tf_op jit(solution)/shard_map/jit(cholesky)/cholesky | solution.py:61
  348.8 1.5 fusion.44
  350.3 9.8 %custom-call.7 = f32[1,128,128]{1,2,0:T(8,128)S(1)} custom-call(f32[1,128,128]{2,1,0:T(8,128)S(1)} %select_bitcast_fusion), custom_call_target="InvertDiagBlocksLowerTriangular" | custom-call | tf_op jit(solution)/shard_map/triangular_solve/custom-call.0 | solution.py:62
  360.1 5.4 %fusion.33 = f32[128,8192]{1,0:T(8,128)S(1)} fusion(f32[128,8192]{1,0:T(8,128)} %copy-done.2, f32[1,128,128]{1,2,0:T(8,128)S(1)} %custom-call.7), kind=kOutput, calls=%fused_computation.38 | convolution fusion | flops 1610612736 | bytes 8454144 | tf_op jit(solution)/shard_map/triangular_solve/dot.1 | solution.py:62
  365.6 3.3 copy.100
  (34 shorter events, 2.6 us)
Async XLA Ops:
  7.2 326.9 %all-reduce.3.cloned.1.call-start = ((), (), s32[]{:S(2)}) async-start(), calls=%async_computation | async-start | bytes 131072 | tf_op jit(solution)/shard_map/psum | solution.py:60
  13.6 4.7 %copy-start.1 = (f32[64,3,4,8,256]{4,0,3,2,1:T(8,128)}, f32[64,3,4,8,256]{4,0,3,2,1:T(8,128)S(1)}, u32[]{:S(2)}) copy-start(f32[64,3,4,8,256]{4,0,3,2,1:T(8,128)S(1)} %copy.65) | copy-start | bytes 18874372
  13.7 8.2 %copy-start = (f32[64,3,4,8,256]{4,3,2,1,0:T(8,128)S(1)}, f32[64,3,4,8,256]{4,3,2,1,0:T(8,128)}, u32[]{:S(2)}) copy-start(f32[64,3,4,8,256]{4,3,2,1,0:T(8,128)} %param.5) | copy-start | bytes 18874372
  18.3 35.8 %collective-permute-start.1 = (f32[64,3,1,8,256]{4,0,3,2,1:T(8,128)}, f32[64,3,1,8,256]{4,0,3,2,1:T(8,128)}, u32[]{:S(2)}, u32[]{:S(2)}) collective-permute-start(f32[64,3,1,8,256]{4,0,3,2,1:T(8,128)} %get-tuple-element.19), channel_id=1, source_target_pairs={{0,4},{4,8},{8,12},{12,16},{16,20},{20,24},{24,28},{28,0},{1,5},{5... | collective-permute-start | bytes 4718600 | tf_op jit(solution)/shard_map/ppermute | solution.py:15
  18.8 43.7 %collective-permute-start = (f32[64,3,1,8,256]{4,0,3,2,1:T(8,128)}, f32[64,3,1,8,256]{4,0,3,2,1:T(8,128)}, u32[]{:S(2)}, u32[]{:S(2)}) collective-permute-start(f32[64,3,1,8,256]{4,0,3,2,1:T(8,128)} %get-tuple-element.18), channel_id=1, source_target_pairs={{4,0},{8,4},{12,8},{16,12},{20,16},{24,20},{28,24},{0,28},{5,1},{9... | collective-permute-start | bytes 4718600 | tf_op jit(solution)/shard_map/ppermute | solution.py:18
  64.1 3.6 copy-start.3
  67.7 7.0 %copy-start.4 = (f32[64,4,8,256]{3,2,1,0:T(8,128)S(1)}, f32[64,4,8,256]{3,2,1,0:T(8,128)}, u32[]{:S(2)}) copy-start(f32[64,4,8,256]{3,2,1,0:T(8,128)} %param.6) | copy-start | bytes 6291460
  69.4 35.6 %collective-permute-start.2 = (f32[64,3,6,1,256]{4,0,3,2,1:T(8,128)}, f32[64,3,6,1,256]{4,0,3,2,1:T(8,128)}, u32[]{:S(2)}, u32[]{:S(2)}) collective-permute-start(f32[64,3,6,1,256]{4,0,3,2,1:T(8,128)} %get-tuple-element.10), channel_id=1, source_target_pairs={{1,0},{2,1},{3,2},{0,3},{5,4},{6,5},{7,6},{4,7},{9,8},{10,9},{11,1... | collective-permute-start | bytes 3538952 | tf_op jit(solution)/shard_map/ppermute | solution.py:18
  74.5 50.2 %collective-permute-start.3 = (f32[64,3,6,1,256]{4,0,3,2,1:T(8,128)}, f32[64,3,6,1,256]{4,0,3,2,1:T(8,128)}, u32[]{:S(2)}, u32[]{:S(2)}) collective-permute-start(f32[64,3,6,1,256]{4,0,3,2,1:T(8,128)} %get-tuple-element.11), channel_id=1, source_target_pairs={{0,1},{1,2},{2,3},{3,0},{4,5},{5,6},{6,7},{7,4},{8,9},{9,10},{10,1... | collective-permute-start | bytes 3538952 | tf_op jit(solution)/shard_map/ppermute | solution.py:15
  85.9 16.4 %slice-start = ((s8[6291456]{0:T(1024)(128)(4,1)}), s8[4194304]{0:T(1024)(128)(4,1)S(1)}, s32[]{:S(2)}) async-start(s8[6291456]{0:T(1024)(128)(4,1)} %bitcast.52), calls=%async_computation.1 | async-start | bytes 8388608
  95.0 7.3 %slice-start.1 = ((s8[6291456]{0:T(1024)(128)(4,1)}), s8[2097152]{0:T(1024)(128)(4,1)S(1)}, s32[]{:S(2)}) async-start(s8[6291456]{0:T(1024)(128)(4,1)} %bitcast.52), calls=%async_computation.2 | async-start | bytes 4194304
  130.1 2.5 copy-start.5
  193.0 155.8 %copy-start.6 = (f32[128,128]{1,0:T(8,128)}, f32[128,128]{1,0:T(8,128)S(1)}, u32[]{:S(2)}) copy-start(f32[128,128]{1,0:T(8,128)S(1)} %get-tuple-element.9) | copy-start | bytes 196612
  210.0 2.0 copy-start.2
Sparse Core Ops, SparseCore 0:
  216.2 117.8 all-reduce.2
where the time goes:
time: 381 us; the launch traced here: 376 us
  waiting for transfers between devices  148 us (39%)
  other arithmetic  74.4 us (20%)
  local copies, waits for them, and re-layouts  64.2 us (17%)
  blocking collectives  41.1 us (11%)
  matrix products  25.3 us (7%)
  between operations  14.6 us (4%)
  starting transfers between devices  8.84 us (2%)
    psum x1, waiting for transfers between devices, shards(): second_sum = lax.psum(product(first_pass, first_pass), ('gx', 'gz'))  118 us
    unnamed x29, local copies, waits for them, and re-layouts  43.8 us
    psum x1, blocking collectives, shards(): lax.psum((product(mode_fields, new_fields), product(new_fields, new_field...  41.1 us
    ppermute x2, waiting for transfers between devices, with_halo(): lax.ppermute(lax.slice_in_dim(block, block.shape[dim] - width, None, axis...  29.5 us
    dot_general x4, matrix products, product(): lax.dot_general(left, right, (((1,), (1,)), ((), ())), precision=precise)  12.8 us
    another operation x3, other arithmetic, shards(): lower_one = jnp.linalg.cholesky(gram_sum / total_cells)  12.4 us
    another operation x3, other arithmetic, shards(): lower_two = jnp.linalg.cholesky(second_sum / total_cells)  12.4 us
    another operation x2, other arithmetic, shards(): lax.linalg.triangular_solve(lower_one, stacked, left_side=True, lower=True)  10.5 us
  transfers between devices with their start and end apart: 5, of which 3 were waited for; matrix products, arithmetic and copies ran while one was open for 16% of the time, Pallas kernels for 0%

commit v1 on v0

v1 whole, which is shorter than its diff:
```python
import functools

import jax
import jax.numpy as jnp
from jax import lax
from jax.experimental import pallas as pl
from jax.experimental.pallas import tpu as pltpu
from jax.sharding import PartitionSpec as P

MESH = pl.DeviceIdType.MESH
F32 = jnp.float32
BF16 = jnp.bfloat16
CHUNKS = 4
PIECES = 32
VMEM_LIMIT = 60 * 1024 * 1024


def split3(x):
    a = x.astype(BF16)
    rest = x - a.astype(F32)
    b = rest.astype(BF16)
    c = (rest - b.astype(F32)).astype(BF16)
    return a, b, c


def split2(x):
    a = x.astype(BF16)
    return a, (x - a.astype(F32)).astype(BF16)


def dot(x, y):
    return lax.dot_general(x, y, (((1,), (0,)), ((), ())), preferred_element_type=F32)


def dot_t(x, y):
    return lax.dot_general(x, y, (((1,), (1,)), ((), ())), preferred_element_type=F32)


def store_pieces(ref, matrix):
    rows = matrix.shape[0] // PIECES
    for i in range(PIECES):
        ref[i] = matrix[i * rows : (i + 1) * rows, :]


def lane_derivative(f):
    width = f.shape[-1]
    lane = lax.broadcasted_iota(jnp.int32, f.shape, 1)
    ahead = pltpu.roll(f, width - 1, 1)
    behind = pltpu.roll(f, 1, 1)
    ahead2 = pltpu.roll(f, width - 2, 1)
    behind2 = pltpu.roll(f, 2, 1)
    inner = ahead - behind
    bottom = -3.0 * f + 4.0 * ahead - ahead2
    top_side = 3.0 * f - 4.0 * behind + behind2
    return 0.5 * jnp.where(lane == 0, bottom, jnp.where(lane == width - 1, top_side, inner))


def halo_kernel(
    nx, nz, vel_hbm, modes_hbm, s_ref, gram_ref,
    vel, crit, modes_split, x_low, x_high, z_low, z_high, z_first, z_last, total,
    load_sem, send_sem, recv_sem,
):
    gx = lax.axis_index("gx")
    gz = lax.axis_index("gz")
    right, left = lax.rem(gx + 1, nx), lax.rem(gx + nx - 1, nx)
    front, back = lax.rem(gz + 1, nz), lax.rem(gz + nz - 1, nz)
    fields, cells_x, cells_z, width = vel_hbm.shape
    snaps = fields // 3
    modes = modes_hbm.shape[0] // (cells_x * cells_z)
    half = width // 2
    per = fields // CHUNKS
    cells = cells_x * cells_z
    group = 8 // cells_x

    def load(j):
        part = pl.ds(j * per, per)
        return pltpu.make_async_copy(vel_hbm.at[part], vel.at[part], load_sem.at[j])

    def load_modes(k):
        src = modes_hbm.at[:, pl.ds(k * half, half)]
        return pltpu.make_async_copy(src, modes_split.at[k], load_sem.at[CHUNKS + k])

    def remote(way, j):
        part = pl.ds(j * per, per)
        rows = pl.ds(j * per * cells_x, per * cells_x)
        src, dst, where = [
            (vel_hbm.at[part, cells_x - 1], x_low.at[part], (right, gz)),
            (vel_hbm.at[part, 0], x_high.at[part], (left, gz)),
            (z_last.at[rows], z_low.at[rows], (gx, front)),
            (z_first.at[rows], z_high.at[rows], (gx, back)),
        ][way]
        return pltpu.make_async_remote_copy(
            src_ref=src, dst_ref=dst, send_sem=send_sem.at[way, j], recv_sem=recv_sem.at[way, j],
            device_id=where, device_id_type=MESH,
        )

    for j in range(CHUNKS):
        load(j).start()
    for k in range(2):
        load_modes(k).start()
    barrier = pltpu.get_barrier_semaphore()
    for where in ((right, gz), (left, gz), (gx, front), (gx, back)):
        pl.semaphore_signal(barrier, inc=1, device_id=where, device_id_type=MESH)
    pl.semaphore_wait(barrier, 4)
    for j in range(CHUNKS):
        remote(0, j).start()
        remote(1, j).start()
    for j in range(CHUNKS):
        load(j).wait()

        @pl.loop(j * per // group, (j + 1) * per // group)
        def _(g):
            rows = pl.ds(pl.multiple_of(g * 8, 8), 8)
            blocks = [vel[g * group + q] for q in range(group)]
            z_first[rows, :] = jnp.concatenate([b[:, 0, :] for b in blocks], axis=0)
            z_last[rows, :] = jnp.concatenate([b[:, cells_z - 1, :] for b in blocks], axis=0)

        remote(2, j).start()
        remote(3, j).start()

    def gather(ref, c, count):
        parts = [ref.at[k][pl.ds(c, count, stride=cells), :] for k in range(2)]
        return jnp.concatenate(parts, axis=1)

    for k in range(2):
        load_modes(k).wait()
    for c in range(cells):
        s_ref[c, 0:modes, :] = gather(modes_split, c, modes)

    def snapshot(s):
        sub = lax.broadcasted_iota(jnp.int32, (cells_z, width), 0)
        u = [[vel[s * 3 + i, x] for x in range(cells_x)] for i in range(3)]
        low = [x_low[s * 3 + i] for i in range(3)]
        high = [x_high[s * 3 + i] for i in range(3)]
        for x in range(cells_x):
            gradx, gradz, grady = [], [], []
            for i in range(3):
                f = u[i][x]
                before = u[i][x - 1] if x > 0 else low[i]
                after = u[i][x + 1] if x < cells_x - 1 else high[i]
                gradx.append((after - before) * 0.5)
                row = pl.ds((s * 3 + i) * cells_x + x, 1)
                under = jnp.where(sub == 0, z_low[row, :], pltpu.roll(f, 1, 0))
                over = jnp.where(sub == cells_z - 1, z_high[row, :], pltpu.roll(f, cells_z - 1, 0))
                gradz.append((over - under) * 0.5)
                grady.append(lane_derivative(f))
            diagonal_part = gradx[0] * gradx[0] + gradz[1] * gradz[1] + grady[2] * grady[2]
            cross_part = gradz[0] * gradx[1] + grady[0] * gradx[2] + grady[1] * gradz[2]
            place = pl.multiple_of((s * cells_x + x) * cells_z, cells_z)
            value = -0.5 * diagonal_part - cross_part
            for k in range(2):
                crit[k, pl.ds(place, cells_z), :] = value[:, k * half : (k + 1) * half]

    for j in range(CHUNKS):
        for way in range(4):
            remote(way, j).wait_recv()

        @pl.loop(j * snaps // CHUNKS, (j + 1) * snaps // CHUNKS)
        def _(s):
            snapshot(s)

    for j in range(CHUNKS):
        for way in range(4):
            remote(way, j).wait_send()

    for c in range(cells):
        s_ref[c, modes:, :] = gather(crit, c, snaps)

    total[...] = jnp.zeros_like(total)

    @pl.loop(0, cells)
    def _(c):
        a, b, d = split3(s_ref[c])
        total[0] += dot_t(a, a) + dot_t(b, b)
        total[1] += dot_t(jnp.concatenate([b, d], axis=1), jnp.concatenate([a, a], axis=1))

    cross = total[1]
    store_pieces(gram_ref, total[0] + (cross + cross.T))


def halo_call(velocity, scaled_modes, nx, nz):
    snaps, _, cells_x, cells_z, width = velocity.shape
    modes = scaled_modes.shape[0]
    fields = snaps * 3
    cells = cells_x * cells_z
    columns = modes + snaps
    x_face = pltpu.VMEM((fields, cells_z, width), F32)
    z_face = pltpu.VMEM((fields * cells_x, width), F32)
    return pl.pallas_call(
        functools.partial(halo_kernel, nx, nz),
        out_shape=(
            jax.ShapeDtypeStruct((cells, columns, width), F32),
            jax.ShapeDtypeStruct((PIECES, columns // PIECES, columns), F32),
        ),
        in_specs=[pl.BlockSpec(memory_space=pl.ANY)] * 2,
        out_specs=[pl.BlockSpec(memory_space=pltpu.VMEM)] * 2,
        scratch_shapes=[
            pltpu.VMEM((fields, cells_x, cells_z, width), F32),
            pltpu.VMEM((2, snaps * cells, width // 2), F32),
            pltpu.VMEM((2, modes * cells, width // 2), F32),
            x_face, x_face, z_face, z_face, z_face, z_face,
            pltpu.VMEM((2, columns, columns), F32),
            pltpu.SemaphoreType.DMA((CHUNKS + 2,)),
            pltpu.SemaphoreType.DMA((4, CHUNKS)),
            pltpu.SemaphoreType.DMA((4, CHUNKS)),
        ],
        compiler_params=pltpu.CompilerParams(
            collective_id=0, has_side_effects=True, vmem_limit_bytes=VMEM_LIMIT
        ),
        name="halo_criterion_gram",
    )(velocity.reshape(fields, cells_x, cells_z, width), scaled_modes.reshape(modes * cells, width))


def reduce_kernel(nx, nz, part_ref, sum_ref, inbox, send_sem, recv_sem, send_two, recv_two):
    count = nx * nz
    owners = min(count, PIECES)
    me = lax.axis_index("gx") * nz + lax.axis_index("gz")

    def place(k):
        return (lax.div(k, nz), lax.rem(k, nz))

    def other(step):
        return lax.rem(me + step, count)

    barrier = pltpu.get_barrier_semaphore()

    @pl.loop(1, count)
    def _(step):
        pl.semaphore_signal(barrier, inc=1, device_id=place(other(step)), device_id_type=MESH)

    pl.semaphore_wait(barrier, count - 1)

    def scatter(k):
        return pltpu.make_async_remote_copy(
            src_ref=part_ref.at[k], dst_ref=inbox.at[me], send_sem=send_sem, recv_sem=recv_sem,
            device_id=place(k), device_id_type=MESH,
        )

    def spread(k):
        return pltpu.make_async_remote_copy(
            src_ref=sum_ref.at[me], dst_ref=sum_ref.at[me], send_sem=send_two, recv_sem=recv_two,
            device_id=place(k), device_id_type=MESH,
        )

    def wait_bytes(ref, number, sem):
        if number:
            view = ref.at[pl.ds(0, number)]
            pltpu.make_async_copy(view, view, sem).wait()

    if owners == count:

        @pl.loop(1, count)
        def _(step):
            scatter(other(step)).start()

        inbox[me] = part_ref[me]
        wait_bytes(inbox, count - 1, recv_sem)
        sum_ref[me] = jnp.sum(inbox[...], axis=0)

        @pl.loop(1, count)
        def _(step):
            spread(other(step)).start()

        wait_bytes(sum_ref, count - 1, recv_two)
        wait_bytes(inbox, count - 1, send_sem)
        wait_bytes(inbox, count - 1, send_two)
    else:
        owner = me < owners

        @pl.loop(0, owners)
        def _(k):
            @pl.when(k != me)
            def _():
                scatter(k).start()

        @pl.when(owner)
        def _():
            inbox[me] = part_ref[me]
            wait_bytes(inbox, count - 1, recv_sem)
            sum_ref[me] = jnp.sum(inbox[...], axis=0)

            @pl.loop(1, count)
            def _(step):
                spread(other(step)).start()

            wait_bytes(sum_ref, owners - 1, recv_two)
            wait_bytes(inbox, owners - 1, send_sem)
            wait_bytes(inbox, count - 1, send_two)

        @pl.when(jnp.logical_not(owner))
        def _():
            wait_bytes(sum_ref, owners, recv_two)
            wait_bytes(inbox, owners, send_sem)


def reduce_call(parts, nx, nz, ident):
    pieces, rows, columns = parts.shape
    return pl.pallas_call(
        functools.partial(reduce_kernel, nx, nz),
        out_shape=jax.ShapeDtypeStruct(parts.shape, F32),
        in_specs=[pl.BlockSpec(memory_space=pltpu.VMEM)],
        out_specs=pl.BlockSpec(memory_space=pltpu.VMEM),
        scratch_shapes=[
            pltpu.VMEM((nx * nz, rows, columns), F32),
            pltpu.SemaphoreType.DMA, pltpu.SemaphoreType.DMA,
            pltpu.SemaphoreType.DMA, pltpu.SemaphoreType.DMA,
        ],
        compiler_params=pltpu.CompilerParams(
            collective_id=ident, has_side_effects=True, vmem_limit_bytes=VMEM_LIMIT
        ),
        name="gram_reduce",
    )(parts)


def factor(tiles, upper_ref, inverse_ref, block=4):
    size = tiles[0].shape[1]
    lane = lax.broadcasted_iota(jnp.int32, (1, size), 1)
    sub = lax.broadcasted_iota(jnp.int32, (8, size), 0)
    for k in range(0, size, block):
        home = k // 8
        off = k % 8
        tile = tiles[home]
        rows = [tile[off + i : off + i + 1, :] for i in range(block)]
        pivot = [
            [tile[off + i : off + i + 1, k + j : k + j + 1] for j in range(block)]
            for i in range(block)
        ]
        inv = []
        for i in range(block):
            inv.append(1.0 / pivot[i][i])
            fixed = jnp.where(lane == k + i, 1.0, rows[i])
            scale = jnp.sqrt(inv[i])
            upper_ref[k + i : k + i + 1, :] = jnp.where(lane >= k + i, rows[i] * scale, 0.0)
            inverse_ref[k + i : k + i + 1, :] = jnp.where(lane <= k + i, fixed * scale, 0.0)
            for j in range(i + 1, block):
                ratio = pivot[i][j] * inv[i]
                rows[j] = jnp.where(lane == k + i, 0.0, rows[j]) - ratio * fixed
                for m in range(j, block):
                    pivot[j][m] = pivot[j][m] - ratio * pivot[i][m]
            rows[i] = fixed
        inside = (lane >= k) & (lane < k + block)
        clear = [jnp.where(inside & (lane > k + i), 0.0, rows[i]) for i in range(block)]
        first = home if off + block < 8 else home + 1
        for t in range(first, len(tiles)):
            tile = tiles[t]
            new = jnp.where(inside, 0.0, tile)
            weights = []
            for i in range(block):
                entry = tile[:, k + i : k + i + 1]
                for m in range(i):
                    entry = entry - weights[m] * pivot[m][i]
                weights.append(entry * inv[i])
                new = new - weights[i] * clear[i]
            tiles[t] = jnp.where(sub >= off + block, new, tile) if t == home else new


def load_tiles(sum_ref, scale):
    rows = sum_ref.shape[1]
    step = 8 // rows
    return [
        jnp.concatenate([sum_ref[t * step + q] for q in range(step)], axis=0) * scale
        for t in range(sum_ref.shape[0] // step)
    ]


def factor_one_kernel(scale, sum_ref, lower_ref, upper_ref, inverse_ref):
    factor(load_tiles(sum_ref, scale), upper_ref, inverse_ref)
    lower_ref[...] = upper_ref[...].T


def factor_two_kernel(scale, sum_ref, upper_one_ref, triangle_ref, inverse_ref, upper_ref):
    factor(load_tiles(sum_ref, scale), upper_ref, inverse_ref)
    triangle_ref[...] = lax.dot_general(
        upper_ref[...], upper_one_ref[...], (((1,), (0,)), ((), ())),
        precision=lax.Precision.HIGHEST, preferred_element_type=F32,
    )


def first_kernel(s_ref, inverse_ref, x_ref, gram_ref, total):
    step = pl.program_id(0)
    wa, wb, wc = split3(inverse_ref[...])
    w_one = jnp.concatenate([wa, wa], axis=1)
    w_two = jnp.concatenate([wb, wb], axis=1)
    w_three = jnp.concatenate([wa, wc], axis=1)

    @pl.when(step == 0)
    def _():
        total[...] = jnp.zeros_like(total)

    same, cross = total[0], total[1]
    for c in range(s_ref.shape[0]):
        sa, sb, sc = split3(s_ref[c])
        pair = jnp.concatenate([sa, sb], axis=0)
        ends = jnp.concatenate([sc, sa], axis=0)
        x = dot(w_one, pair) + (dot(w_two, pair) + dot(w_three, ends))
        x_ref[c] = x
        a, b = split2(x)
        same = same + dot_t(a, a)
        cross = cross + dot_t(b, a)
    total[0] = same
    total[1] = cross

    @pl.when(step == pl.num_programs(0) - 1)
    def _():
        store_pieces(gram_ref, total[0] + (total[1] + total[1].T))


def second_kernel(x_ref, inverse_ref, out_ref):
    wa, wb = split2(inverse_ref[...])
    w_all = jnp.concatenate([wa, wa, wb], axis=1)
    columns, _, width = out_ref.shape
    for c in range(x_ref.shape[0]):
        a, b = split2(x_ref[c])
        out_ref[:, c, :] = dot(w_all, jnp.concatenate([a, b, a], axis=0))


def shards(velocity, scaled_modes):
    snaps, _, cells_x, cells_z, width = velocity.shape
    columns = scaled_modes.shape[0] + snaps
    nx, nz = lax.axis_size("gx"), lax.axis_size("gz")
    cells = cells_x * cells_z
    scale = 1.0 / (cells * nx * nz * width)
    square = jax.ShapeDtypeStruct((columns, columns), F32)
    whole = pl.BlockSpec(memory_space=pltpu.VMEM)
    params = pltpu.CompilerParams(vmem_limit_bytes=VMEM_LIMIT)

    stacked, part_one = halo_call(velocity, scaled_modes, nx, nz)
    sum_one = reduce_call(part_one, nx, nz, 1)
    lower_one, upper_one, inverse_one = pl.pallas_call(
        functools.partial(factor_one_kernel, scale),
        out_shape=(square, square, square), in_specs=[whole], out_specs=[whole] * 3,
        compiler_params=params, name="factor_one",
    )(sum_one)
    group = 4
    block = pl.BlockSpec((group, columns, width), lambda i: (i, 0, 0))
    still = pl.BlockSpec((columns, columns), lambda i: (0, 0))
    first_pass, part_two = pl.pallas_call(
        first_kernel,
        grid=(cells // group,),
        out_shape=(
            jax.ShapeDtypeStruct(stacked.shape, F32),
            jax.ShapeDtypeStruct(part_one.shape, F32),
        ),
        in_specs=[block, still],
        out_specs=[block, pl.BlockSpec(part_one.shape, lambda i: (0, 0, 0))],
        scratch_shapes=[pltpu.VMEM((2, columns, columns), F32)],
        compiler_params=params, name="first_pass",
    )(stacked, inverse_one)
    sum_two = reduce_call(part_two, nx, nz, 2)
    triangle, inverse_two = pl.pallas_call(
        functools.partial(factor_two_kernel, scale),
        out_shape=(square, square), in_specs=[whole] * 2, out_specs=[whole] * 2,
        scratch_shapes=[pltpu.VMEM((columns, columns), F32)],
        compiler_params=params, name="factor_two",
    )(sum_two, upper_one)
    basis = pl.pallas_call(
        second_kernel,
        grid=(cells_x,),
        out_shape=jax.ShapeDtypeStruct((columns, cells, width), F32),
        in_specs=[pl.BlockSpec((cells_z, columns, width), lambda i: (i, 0, 0)), still],
        out_specs=pl.BlockSpec((columns, cells_z, width), lambda i: (0, i, 0)),
        compiler_params=params, name="second_pass",
    )(first_pass, inverse_two)
    return (basis.reshape(columns, cells_x, cells_z, width), triangle, lower_one)


def solution(mesh):
    in_specs = (P(None, None, "gx", "gz", None), P(None, "gx", "gz", None))
    out_specs = (P(None, "gx", "gz", None), P(), P())
    return jax.shard_map(shards, mesh=mesh, in_specs=in_specs, out_specs=out_specs, check_vma=False)
```

time: 381 us -> 136 us (0.36); the launches traced: 376 us -> 135 us
  waiting for transfers between devices: 148 us -> 0 us
  Pallas kernels: 0 us -> 134 us
  other arithmetic: 74.4 us -> 0 us
  local copies, waits for them, and re-layouts: 64.2 us -> 0 us
  blocking collectives: 41.1 us -> 0 us
  matrix products: 25.3 us -> 0 us
  between operations: 14.6 us -> 0.66 us
  starting transfers between devices: 8.84 us -> 0 us
    pallas_call x0 -> x7, Pallas kernels: none -> 134 us  [the longest x1 54.7 us: halo_call(): pl.pallas_call(functools.partial(halo_kernel, nx, nz), out_shape=(jax.Sha...]
    psum x1 -> x0, waiting for transfers between devices: 118 us -> none  [shards(): second_sum = lax.psum(product(first_pass, first_pass), ('gx', 'gz'))]
    another operation x10 -> x0, other arithmetic: 45.6 us -> none  [the longest x3 12.4 us: shards(): lower_one = jnp.linalg.cholesky(gram_sum / total_cells)]
    unnamed x29 -> x0, local copies, waits for them, and re-layouts: 43.8 us -> none
    psum x1 -> x0, blocking collectives: 41.1 us -> none  [shards(): lax.psum((product(mode_fields, new_fields), product(new_fields, new_field...]
    ppermute x4 -> x0, waiting for transfers between devices: 29.5 us -> none  [the longest x2 29.5 us: with_halo(): lax.ppermute(lax.slice_in_dim(block, block.shape[dim] - width, None, axis...]
    mul x5 -> x0, other arithmetic: 17.2 us -> none  [the longest x1 9.14 us: along_wall(): inner = (field[..., 2:] - field[..., :-2]) * 0.5]
    dot_general x5 -> x0, matrix products: 14.3 us -> none  [the longest x4 12.8 us: product(): lax.dot_general(left, right, (((1,), (1,)), ((), ())), precision=precise)]
  transfers between devices with their start and end apart: 5 -> 0, of which waited for: 3 -> 0; matrix products, arithmetic and copies ran while one was open for 16% -> 0% of each run, Pallas kernels for 0% -> 0%
where the time goes in v1:
time: 136 us; the launch traced here: 135 us
  Pallas kernels  134 us (99%)
    pallas_call x1, Pallas kernels, halo_call(): pl.pallas_call(functools.partial(halo_kernel, nx, nz), out_shape=(jax.Sha...  54.7 us
    pallas_call x2, Pallas kernels, reduce_call(): pl.pallas_call(functools.partial(reduce_kernel, nx, nz), out_shape=jax.Sh...  27.6 us
    pallas_call x1, Pallas kernels, shards(): pl.pallas_call(functools.partial(factor_two_kernel, scale), out_shape=(sq...  17.4 us
    pallas_call x1, Pallas kernels, shards(): pl.pallas_call(functools.partial(factor_one_kernel, scale), out_shape=(sq...  17.3 us
    pallas_call x1, Pallas kernels, shards(): pl.pallas_call(first_kernel, grid=(cells // group,), out_shape=(jax.Shape...  11.4 us
    pallas_call x1, Pallas kernels, shards(): pl.pallas_call(second_kernel, grid=(cells_x,), out_shape=jax.ShapeDtypeSt...  5.81 us

profile of v1, /device:TPU:0, one launch (start us, length us, event | category | flops | bytes accessed | tf_op | source)
XLA Modules:
  0.0 135.0 jit_solution(18171901898036143496)
XLA Ops:
  0.6 54.7 %halo_criterion_gram.1 = (f32[32,128,256]{2,1,0:T(8,128)}, f32[32,4,128]{2,1,0:T(4,128)}) custom-call(f32[192,4,8,256]{3,2,1,0:T(8,128)} %bitcast.3, f32[2048,256]{1,0:T(8,128)} %bitcast.5), custom_call_target="tpu_custom_call" | custom-call | tf_op jit(solution)/shard_map/halo_criterion_gram/pallas_call | solution.py:189
  55.4 15.4 %gram_reduce.2.sum_ref = f32[32,4,128]{2,1,0:T(4,128)} custom-call(f32[32,4,128]{2,1,0:T(4,128)} %get-tuple-element.13.part_ref), custom_call_target="tpu_custom_call" | custom-call | tf_op jit(solution)/shard_map/gram_reduce/pallas_call | solution.py:298
  70.8 17.3 %factor_one.1 = (f32[128,128]{1,0:T(8,128)}, f32[128,128]{1,0:T(8,128)}, f32[128,128]{1,0:T(8,128)}) custom-call(f32[32,4,128]{2,1,0:T(4,128)} %gram_reduce.2.sum_ref), custom_call_target="tpu_custom_call" | custom-call | tf_op jit(solution)/shard_map/factor_one/pallas_call | solution.py:429
  88.1 11.4 %first_pass.1 = (f32[32,128,256]{2,1,0:T(8,128)}, f32[32,4,128]{2,1,0:T(4,128)}) custom-call(f32[32,128,256]{2,1,0:T(8,128)} %get-tuple-element.12.s_ref, f32[128,128]{1,0:T(8,128)} %get-tuple-element.14.inverse_ref), custom_call_target="tpu_custom_call" | custom-call | tf_op jit(solution)/shard_map/first_pass/pallas_call | solution.py:437
  99.5 12.2 %gram_reduce.3.sum_ref = f32[32,4,128]{2,1,0:T(4,128)} custom-call(f32[32,4,128]{2,1,0:T(4,128)} %get-tuple-element.16.part_ref), custom_call_target="tpu_custom_call" | custom-call | tf_op jit(solution)/shard_map/gram_reduce/pallas_call | solution.py:298
  111.7 17.4 %factor_two.1 = (f32[128,128]{1,0:T(8,128)}, f32[128,128]{1,0:T(8,128)}) custom-call(f32[32,4,128]{2,1,0:T(4,128)} %gram_reduce.3.sum_ref, f32[128,128]{1,0:T(8,128)} %get-tuple-element.17.upper_one_ref), custom_call_target="tpu_custom_call" | custom-call | tf_op jit(solution)/shard_map/factor_two/pallas_call | solution.py:450
  129.1 5.8 %second_pass.1 = f32[128,32,256]{2,1,0:T(8,128)} custom-call(f32[32,128,256]{2,1,0:T(8,128)} %get-tuple-element.15.x_ref, f32[128,128]{1,0:T(8,128)} %get-tuple-element.18.inverse_ref), custom_call_target="tpu_custom_call" | custom-call | tf_op jit(solution)/shard_map/second_pass/pallas_call | solution.py:456

commit v2 on v1

v2 whole, which is shorter than its diff:
```python
import functools

import jax
import jax.numpy as jnp
from jax import lax
from jax.experimental import pallas as pl
from jax.experimental.pallas import tpu as pltpu
from jax.sharding import PartitionSpec as P

MESH = pl.DeviceIdType.MESH
F32 = jnp.float32
BF16 = jnp.bfloat16
CHUNKS = 8
PIECES = 32
VMEM_LIMIT = 60 * 1024 * 1024


def split3(x):
    a = x.astype(BF16)
    rest = x - a.astype(F32)
    b = rest.astype(BF16)
    c = (rest - b.astype(F32)).astype(BF16)
    return a, b, c


def split2(x):
    a = x.astype(BF16)
    return a, (x - a.astype(F32)).astype(BF16)


def dot(x, y):
    return lax.dot_general(x, y, (((1,), (0,)), ((), ())), preferred_element_type=F32)


def dot_t(x, y):
    return lax.dot_general(x, y, (((1,), (1,)), ((), ())), preferred_element_type=F32)


def store_pieces(ref, matrix):
    rows = matrix.shape[0] // PIECES
    for i in range(PIECES):
        ref[i] = matrix[i * rows : (i + 1) * rows, :]


def lane_derivative(f):
    width = f.shape[-1]
    lane = lax.broadcasted_iota(jnp.int32, f.shape, 1)
    ahead = pltpu.roll(f, width - 1, 1)
    behind = pltpu.roll(f, 1, 1)
    ahead2 = pltpu.roll(f, width - 2, 1)
    behind2 = pltpu.roll(f, 2, 1)
    inner = ahead - behind
    bottom = -3.0 * f + 4.0 * ahead - ahead2
    top_side = 3.0 * f - 4.0 * behind + behind2
    return 0.5 * jnp.where(lane == 0, bottom, jnp.where(lane == width - 1, top_side, inner))


def halo_kernel(
    nx, nz, vel_hbm, modes_hbm, s_ref, sum_ref,
    vel, crit, modes_split, x_low, x_high, z_low, z_high, z_first, z_last, total,
    load_sem, send_sem, recv_sem, part, inbox, reduce_sems,
):
    gx = lax.axis_index("gx")
    gz = lax.axis_index("gz")
    right, left = lax.rem(gx + 1, nx), lax.rem(gx + nx - 1, nx)
    front, back = lax.rem(gz + 1, nz), lax.rem(gz + nz - 1, nz)
    fields, cells_x, cells_z, width = vel_hbm.shape
    snaps = fields // 3
    modes = modes_hbm.shape[0] // (cells_x * cells_z)
    half = width // 2
    per = fields // CHUNKS
    cells = cells_x * cells_z
    group = 8 // cells_x

    def load(j):
        part = pl.ds(j * per, per)
        return pltpu.make_async_copy(vel_hbm.at[part], vel.at[part], load_sem.at[j])

    def load_modes(k):
        src = modes_hbm.at[:, pl.ds(k * half, half)]
        return pltpu.make_async_copy(src, modes_split.at[k], load_sem.at[CHUNKS + k])

    def remote(way, j):
        part = pl.ds(j * per, per)
        rows = pl.ds(j * per * cells_x, per * cells_x)
        src, dst, where = [
            (vel_hbm.at[part, cells_x - 1], x_low.at[part], (right, gz)),
            (vel_hbm.at[part, 0], x_high.at[part], (left, gz)),
            (z_last.at[rows], z_low.at[rows], (gx, front)),
            (z_first.at[rows], z_high.at[rows], (gx, back)),
        ][way]
        return pltpu.make_async_remote_copy(
            src_ref=src, dst_ref=dst, send_sem=send_sem.at[way, j], recv_sem=recv_sem.at[way, j],
            device_id=where, device_id_type=MESH,
        )

    greet(nx, nz)
    for j in range(CHUNKS):
        load(j).start()
    for k in range(2):
        load_modes(k).start()
    pl.semaphore_wait(pltpu.get_barrier_semaphore(), nx * nz - 1)
    for j in range(CHUNKS):
        remote(0, j).start()
        remote(1, j).start()
    for j in range(CHUNKS):
        load(j).wait()

        @pl.loop(j * per // group, (j + 1) * per // group)
        def _(g):
            rows = pl.ds(pl.multiple_of(g * 8, 8), 8)
            blocks = [vel[g * group + q] for q in range(group)]
            z_first[rows, :] = jnp.concatenate([b[:, 0, :] for b in blocks], axis=0)
            z_last[rows, :] = jnp.concatenate([b[:, cells_z - 1, :] for b in blocks], axis=0)

        remote(2, j).start()
        remote(3, j).start()

    def gather(ref, c, count):
        parts = [ref.at[k][pl.ds(c, count, stride=cells), :] for k in range(2)]
        return jnp.concatenate(parts, axis=1)

    for k in range(2):
        load_modes(k).wait()
    for c in range(cells):
        s_ref[c, 0:modes, :] = gather(modes_split, c, modes)

    def snapshot(s):
        sub = lax.broadcasted_iota(jnp.int32, (cells_z, width), 0)
        u = [[vel[s * 3 + i, x] for x in range(cells_x)] for i in range(3)]
        low = [x_low[s * 3 + i] for i in range(3)]
        high = [x_high[s * 3 + i] for i in range(3)]
        for x in range(cells_x):
            gradx, gradz, grady = [], [], []
            for i in range(3):
                f = u[i][x]
                before = u[i][x - 1] if x > 0 else low[i]
                after = u[i][x + 1] if x < cells_x - 1 else high[i]
                gradx.append((after - before) * 0.5)
                row = pl.ds((s * 3 + i) * cells_x + x, 1)
                under = jnp.where(sub == 0, z_low[row, :], pltpu.roll(f, 1, 0))
                over = jnp.where(sub == cells_z - 1, z_high[row, :], pltpu.roll(f, cells_z - 1, 0))
                gradz.append((over - under) * 0.5)
                grady.append(lane_derivative(f))
            diagonal_part = gradx[0] * gradx[0] + gradz[1] * gradz[1] + grady[2] * grady[2]
            cross_part = gradz[0] * gradx[1] + grady[0] * gradx[2] + grady[1] * gradz[2]
            place = pl.multiple_of((s * cells_x + x) * cells_z, cells_z)
            value = -0.5 * diagonal_part - cross_part
            for k in range(2):
                crit[k, pl.ds(place, cells_z), :] = value[:, k * half : (k + 1) * half]

    few = snaps // CHUNKS
    for j in range(CHUNKS):
        for way in range(4):
            remote(way, j).wait_recv()

        @pl.loop(j * few, (j + 1) * few)
        def _(s):
            snapshot(s)

        for c in range(cells):
            got = [crit.at[k][pl.ds(j * few * cells + c, few, stride=cells), :] for k in range(2)]
            s_ref[c, modes + j * few : modes + (j + 1) * few, :] = jnp.concatenate(got, axis=1)

    total[...] = jnp.zeros_like(total)
    columns = s_ref.shape[1]

    @pl.loop(0, cells // 4)
    def _(g):
        pieces = [split3(s_ref[g * 4 + q]) for q in range(4)]
        a, b, d = [jnp.concatenate(kind, axis=1) for kind in zip(*pieces)]
        total[0:columns] += dot_t(b, b)
        total[columns:] += dot_t(jnp.concatenate([a, b, d], axis=0), a)

    cross = total[2 * columns : 3 * columns] + total[3 * columns :]
    store_pieces(part, total[columns : 2 * columns] + (total[0:columns] + (cross + cross.T)))
    for j in range(CHUNKS):
        for way in range(4):
            remote(way, j).wait_send()
    reduce_all(nx, nz, part, sum_ref, inbox, reduce_sems)


def halo_call(velocity, scaled_modes, nx, nz):
    snaps, _, cells_x, cells_z, width = velocity.shape
    modes = scaled_modes.shape[0]
    fields = snaps * 3
    cells = cells_x * cells_z
    columns = modes + snaps
    x_face = pltpu.VMEM((fields, cells_z, width), F32)
    z_face = pltpu.VMEM((fields * cells_x, width), F32)
    return pl.pallas_call(
        functools.partial(halo_kernel, nx, nz),
        out_shape=(
            jax.ShapeDtypeStruct((cells, columns, width), F32),
            jax.ShapeDtypeStruct((PIECES, columns // PIECES, columns), F32),
        ),
        in_specs=[pl.BlockSpec(memory_space=pl.ANY)] * 2,
        out_specs=[pl.BlockSpec(memory_space=pltpu.VMEM)] * 2,
        scratch_shapes=[
            pltpu.VMEM((fields, cells_x, cells_z, width), F32),
            pltpu.VMEM((2, snaps * cells, width // 2), F32),
            pltpu.VMEM((2, modes * cells, width // 2), F32),
            x_face, x_face, z_face, z_face, z_face, z_face,
            pltpu.VMEM((4 * columns, columns), F32),
            pltpu.SemaphoreType.DMA((CHUNKS + 2,)),
            pltpu.SemaphoreType.DMA((4, CHUNKS)),
            pltpu.SemaphoreType.DMA((4, CHUNKS)),
            *reduce_scratch(nx * nz, columns),
        ],
        compiler_params=pltpu.CompilerParams(
            collective_id=0, has_side_effects=True, vmem_limit_bytes=VMEM_LIMIT
        ),
        name="halo_criterion_gram",
    )(velocity.reshape(fields, cells_x, cells_z, width), scaled_modes.reshape(modes * cells, width))


def greet(nx, nz):
    gx, gz = lax.axis_index("gx"), lax.axis_index("gz")
    barrier = pltpu.get_barrier_semaphore()
    for dx, dz in other_steps(nx, nz):
        where = (lax.rem(gx + dx, nx), lax.rem(gz + dz, nz))
        pl.semaphore_signal(barrier, inc=1, device_id=where, device_id_type=MESH)


def other_steps(nx, nz):
    return [(dx, dz) for dx in range(nx) for dz in range(nz) if dx or dz]


def reduce_all(nx, nz, part_ref, sum_ref, inbox, sems):
    send_sem, recv_sem, send_two, recv_two = [sems.at[i] for i in range(4)]
    count = nx * nz
    owners = min(count, PIECES)
    gx, gz = lax.axis_index("gx"), lax.axis_index("gz")
    me = gx * nz + gz

    def target(dx, dz):
        return lax.rem(gx + dx, nx), lax.rem(gz + dz, nz)

    def scatter(where):
        return pltpu.make_async_remote_copy(
            src_ref=part_ref.at[where[0] * nz + where[1]], dst_ref=inbox.at[me],
            send_sem=send_sem, recv_sem=recv_sem, device_id=where, device_id_type=MESH,
        )

    def spread(where):
        return pltpu.make_async_remote_copy(
            src_ref=sum_ref.at[me], dst_ref=sum_ref.at[me], send_sem=send_two, recv_sem=recv_two,
            device_id=where, device_id_type=MESH,
        )

    def wait_bytes(ref, number, sem):
        if number:
            view = ref.at[pl.ds(0, number)]
            pltpu.make_async_copy(view, view, sem).wait()

    def add_up():
        inbox[me] = part_ref[me]
        wait_bytes(inbox, count - 1, recv_sem)
        sum_ref[me] = jnp.sum(inbox[...], axis=0)

    if owners == count:
        for step in other_steps(nx, nz):
            scatter(target(*step)).start()
        add_up()
        for step in other_steps(nx, nz):
            spread(target(*step)).start()
        wait_bytes(sum_ref, count - 1, recv_two)
        wait_bytes(inbox, count - 1, send_sem)
        wait_bytes(inbox, count - 1, send_two)
    else:
        owner = me < owners

        @pl.loop(0, owners)
        def _(k):
            @pl.when(k != me)
            def _():
                scatter((lax.div(k, nz), lax.rem(k, nz))).start()

        @pl.when(owner)
        def _():
            add_up()

            @pl.loop(1, count)
            def _(step):
                k = lax.rem(me + step, count)
                spread((lax.div(k, nz), lax.rem(k, nz))).start()

            wait_bytes(sum_ref, owners - 1, recv_two)
            wait_bytes(inbox, owners - 1, send_sem)
            wait_bytes(inbox, count - 1, send_two)

        @pl.when(jnp.logical_not(owner))
        def _():
            wait_bytes(sum_ref, owners, recv_two)
            wait_bytes(inbox, owners, send_sem)


def reduce_scratch(count, columns):
    rows = columns // PIECES
    return [
        pltpu.VMEM((PIECES, rows, columns), F32),
        pltpu.VMEM((count, rows, columns), F32),
        pltpu.SemaphoreType.DMA((4,)),
    ]


def factor(tiles, upper_ref, inverse_ref):
    size = tiles[0].shape[1]
    shape = (8, size)
    lane = lax.broadcasted_iota(jnp.int32, shape, 1)
    sub = lax.broadcasted_iota(jnp.int32, shape, 0)
    for home in range(len(tiles)):
        k = home * 8
        tile = tiles[home]
        rows = [jnp.broadcast_to(tile[i : i + 1, :], shape) for i in range(8)]
        pivot = [
            [jnp.broadcast_to(rows[i][:, k + j : k + j + 1], shape) if j >= i else None for j in range(8)]
            for i in range(8)
        ]
        inv = []
        upper = jnp.zeros(shape, F32)
        inverse = jnp.zeros(shape, F32)
        for i in range(8):
            inv.append(1.0 / pivot[i][i])
            fixed = jnp.where(lane == k + i, 1.0, rows[i])
            scale = jnp.sqrt(inv[i])
            upper = jnp.where((sub == i) & (lane >= k + i), rows[i] * scale, upper)
            inverse = jnp.where((sub == i) & (lane <= k + i), fixed * scale, inverse)
            for j in range(i + 1, 8):
                ratio = pivot[i][j] * inv[i]
                rows[j] = jnp.where(lane == k + i, 0.0, rows[j]) - ratio * fixed
                for m in range(j, 8):
                    pivot[j][m] = pivot[j][m] - ratio * pivot[i][m]
            rows[i] = fixed
        upper_ref[k : k + 8, :] = upper
        inverse_ref[k : k + 8, :] = inverse
        inside = (lane >= k) & (lane < k + 8)
        clear = [jnp.where(inside & (lane > k + i), 0.0, rows[i]) for i in range(8)]
        for t in range(home + 1, len(tiles)):
            tile = tiles[t]
            new = jnp.where(inside, 0.0, tile)
            weights = []
            for i in range(8):
                entry = jnp.broadcast_to(tile[:, k + i : k + i + 1], shape)
                for m in range(i):
                    entry = entry - weights[m] * pivot[m][i]
                weights.append(entry * inv[i])
                new = new - weights[i] * clear[i]
            tiles[t] = new


def load_tiles(sum_ref, scale):
    rows = sum_ref.shape[1]
    step = 8 // rows
    return [
        jnp.concatenate([sum_ref[t * step + q] for q in range(step)], axis=0) * scale
        for t in range(sum_ref.shape[0] // step)
    ]


def factor_one_kernel(scale, sum_ref, lower_ref, upper_ref, inverse_ref):
    factor(load_tiles(sum_ref, scale), upper_ref, inverse_ref)
    lower_ref[...] = upper_ref[...].T


def first_kernel(nx, nz, s_ref, inverse_ref, x_ref, sum_ref, total, part, inbox, reduce_sems):
    greet(nx, nz)
    wa, wb, wc = split3(inverse_ref[...])
    columns = wa.shape[0]
    main = jnp.concatenate(
        [
            jnp.concatenate([wa, wa], axis=1),
            jnp.concatenate([wb, wb], axis=1),
            jnp.concatenate([wc, jnp.zeros_like(wc)], axis=1),
        ],
        axis=0,
    )
    total[...] = jnp.zeros_like(total)

    @pl.loop(0, s_ref.shape[0] // 4)
    def _(g):
        high, low = [], []
        for q in range(4):
            sa, sb, sc = split3(s_ref[g * 4 + q])
            y = dot(main, jnp.concatenate([sa, sb], axis=0))
            x = y[0:columns] + (y[columns : 2 * columns] + y[2 * columns :] + dot(wa, sc))
            x_ref[g * 4 + q] = x
            a, b = split2(x)
            high.append(a)
            low.append(b)
        a = jnp.concatenate(high, axis=1)
        total[...] += dot_t(jnp.concatenate([a, jnp.concatenate(low, axis=1)], axis=0), a)

    cross = total[columns:]
    store_pieces(part, total[0:columns] + (cross + cross.T))
    pl.semaphore_wait(pltpu.get_barrier_semaphore(), nx * nz - 1)
    reduce_all(nx, nz, part, sum_ref, inbox, reduce_sems)


def second_kernel(
    scale, x_ref, sum_ref, upper_one_ref, out_ref, triangle_ref, inverse_ref, upper_ref
):
    @pl.when(pl.program_id(0) == 0)
    def _():
        factor(load_tiles(sum_ref, scale), upper_ref, inverse_ref)
        triangle_ref[...] = lax.dot_general(
            upper_ref[...], upper_one_ref[...], (((1,), (0,)), ((), ())),
            precision=lax.Precision.HIGHEST, preferred_element_type=F32,
        )

    wa, wb = split2(inverse_ref[...])
    columns, _, width = out_ref.shape
    both = jnp.concatenate(
        [jnp.concatenate([wa, wa], axis=1), jnp.concatenate([wb, jnp.zeros_like(wb)], axis=1)],
        axis=0,
    )
    for c in range(x_ref.shape[0]):
        y = dot(both, jnp.concatenate(split2(x_ref[c]), axis=0))
        out_ref[:, c, :] = y[0:columns] + y[columns:]


def shards(velocity, scaled_modes):
    snaps, _, cells_x, cells_z, width = velocity.shape
    columns = scaled_modes.shape[0] + snaps
    nx, nz = lax.axis_size("gx"), lax.axis_size("gz")
    cells = cells_x * cells_z
    scale = 1.0 / (cells * nx * nz * width)
    square = jax.ShapeDtypeStruct((columns, columns), F32)
    whole = pl.BlockSpec(memory_space=pltpu.VMEM)
    params = pltpu.CompilerParams(vmem_limit_bytes=VMEM_LIMIT)

    stacked, sum_one = halo_call(velocity, scaled_modes, nx, nz)
    lower_one, upper_one, inverse_one = pl.pallas_call(
        functools.partial(factor_one_kernel, scale),
        out_shape=(square, square, square), in_specs=[whole], out_specs=[whole] * 3,
        compiler_params=params, name="factor_one",
    )(sum_one)
    first_pass, sum_two = pl.pallas_call(
        functools.partial(first_kernel, nx, nz),
        out_shape=(
            jax.ShapeDtypeStruct(stacked.shape, F32),
            jax.ShapeDtypeStruct(sum_one.shape, F32),
        ),
        in_specs=[whole] * 2,
        out_specs=[whole] * 2,
        scratch_shapes=[
            pltpu.VMEM((2 * columns, columns), F32), *reduce_scratch(nx * nz, columns)
        ],
        compiler_params=pltpu.CompilerParams(
            collective_id=1, has_side_effects=True, vmem_limit_bytes=VMEM_LIMIT
        ),
        name="first_pass_gram",
    )(stacked, inverse_one)
    still = pl.BlockSpec((columns, columns), lambda i: (0, 0))
    basis, triangle = pl.pallas_call(
        functools.partial(second_kernel, scale),
        grid=(cells_x,),
        out_shape=(jax.ShapeDtypeStruct((columns, cells, width), F32), square),
        in_specs=[
            pl.BlockSpec((cells_z, columns, width), lambda i: (i, 0, 0)),
            pl.BlockSpec(sum_two.shape, lambda i: (0, 0, 0)),
            still,
        ],
        out_specs=[pl.BlockSpec((columns, cells_z, width), lambda i: (0, i, 0)), still],
        scratch_shapes=[pltpu.VMEM((columns, columns), F32)] * 2,
        compiler_params=params, name="second_pass",
    )(first_pass, sum_two, upper_one)
    return (basis.reshape(columns, cells_x, cells_z, width), triangle, lower_one)


def solution(mesh):
    in_specs = (P(None, None, "gx", "gz", None), P(None, "gx", "gz", None))
    out_specs = (P(None, "gx", "gz", None), P(), P())
    return jax.shard_map(shards, mesh=mesh, in_specs=in_specs, out_specs=out_specs, check_vma=False)
```

time: 136 us -> 96.2 us (0.71)
  Pallas kernels: 134 us -> 95.3 us
    pallas_call x5 -> x2, Pallas kernels: 62.3 us -> 29.5 us  [the longest x1 19.1 us: shards(): pl.pallas_call(functools.partial(first_kernel, nx, nz), out_shape=(jax.Sh...]
    pallas_call x1, Pallas kernels: 17.3 us -> 5.54 us  [shards(): pl.pallas_call(functools.partial(factor_one_kernel, scale), out_shape=(sq...]
    pallas_call x1, Pallas kernels: 54.7 us -> 60.3 us  [halo_call(): pl.pallas_call(functools.partial(halo_kernel, nx, nz), out_shape=(jax.Sha...]
where the time goes in v2:
time: 96.2 us; the launch traced here: 95.9 us
  Pallas kernels  95.3 us (99%)
    pallas_call x1, Pallas kernels, halo_call(): pl.pallas_call(functools.partial(halo_kernel, nx, nz), out_shape=(jax.Sha...  60.3 us
    pallas_call x1, Pallas kernels, shards(): pl.pallas_call(functools.partial(first_kernel, nx, nz), out_shape=(jax.Sh...  19.1 us
    pallas_call x1, Pallas kernels, shards(): pl.pallas_call(functools.partial(second_kernel, scale), grid=(cells_x,),...  10.4 us
    pallas_call x1, Pallas kernels, shards(): pl.pallas_call(functools.partial(factor_one_kernel, scale), out_shape=(sq...  5.54 us

profile of v2, /device:TPU:0, one launch (start us, length us, event | category | flops | bytes accessed | tf_op | source)
XLA Modules:
  0.0 95.9 jit_solution(1965573900624140586)
XLA Ops:
  0.6 60.3 %halo_criterion_gram.1 = (f32[32,128,256]{2,1,0:T(8,128)}, f32[32,4,128]{2,1,0:T(4,128)}) custom-call(f32[192,4,8,256]{3,2,1,0:T(8,128)} %bitcast.3, f32[2048,256]{1,0:T(8,128)} %bitcast.4), custom_call_target="tpu_custom_call" | custom-call | tf_op jit(solution)/shard_map/halo_criterion_gram/pallas_call | solution.py:191
  60.9 5.5 %factor_one.1 = (f32[128,128]{1,0:T(8,128)}, f32[128,128]{1,0:T(8,128)}, f32[128,128]{1,0:T(8,128)}) custom-call(f32[32,4,128]{2,1,0:T(4,128)} %get-tuple-element.13.sum_ref), custom_call_target="tpu_custom_call" | custom-call | tf_op jit(solution)/shard_map/factor_one/pallas_call | solution.py:433
  66.5 19.1 %first_pass_gram.1 = (f32[32,128,256]{2,1,0:T(8,128)}, f32[32,4,128]{2,1,0:T(4,128)}) custom-call(f32[32,128,256]{2,1,0:T(8,128)} %get-tuple-element.12.s_ref, f32[128,128]{1,0:T(8,128)} %get-tuple-element.14.inverse_ref), custom_call_target="tpu_custom_call" | custom-call | tf_op jit(solution)/shard_map/first_pass_gram/pallas_call | solution.py:438
  85.5 10.4 %second_pass.1 = (f32[128,32,256]{2,1,0:T(8,128)}, f32[128,128]{1,0:T(8,128)}) custom-call(f32[32,128,256]{2,1,0:T(8,128)} %get-tuple-element.15.x_ref, f32[32,4,128]{2,1,0:T(4,128)} %get-tuple-element.16.sum_ref, f32[128,128]{1,0:T(8,128)} %get-tuple-element.17.upper_one_ref), custom_call_target="tpu_custom_call" | custom-call | tf_op jit(solution)/shard_map/second_pass/pallas_call | solution.py:455

commit v3 on v2

--- a/solution.py
+++ b/solution.py
@@ -11,6 +11,8 @@
 F32 = jnp.float32
 BF16 = jnp.bfloat16
 CHUNKS = 8
+WINDOW = 3
+GROUP = 8
 PIECES = 32
 VMEM_LIMIT = 60 * 1024 * 1024
 
@@ -56,9 +58,9 @@
 
 
 def halo_kernel(
-    nx, nz, vel_hbm, modes_hbm, s_ref, sum_ref,
-    vel, crit, modes_split, x_low, x_high, z_low, z_high, z_first, z_last, total,
-    load_sem, send_sem, recv_sem, part, inbox, reduce_sems,
+    nx, nz, scale, vel_hbm, modes_hbm, x_hbm, sum_two_ref, upper_ref,
+    s_ref, x_ref, inverse_ref, sum_ref, vel, crit, modes_split, x_low, x_high, z_low, z_high, z_first, z_last, total,
+    load_sem, send_sem, recv_sem, part, inbox, reduce_sems, part_two, inbox_two, reduce_two,
 ):
     gx = lax.axis_index("gx")
     gz = lax.axis_index("gz")
@@ -100,10 +102,9 @@
     for k in range(2):
         load_modes(k).start()
     pl.semaphore_wait(pltpu.get_barrier_semaphore(), nx * nz - 1)
-    for j in range(CHUNKS):
+    def send(j):
         remote(0, j).start()
         remote(1, j).start()
-    for j in range(CHUNKS):
         load(j).wait()
 
         @pl.loop(j * per // group, (j + 1) * per // group)
@@ -115,6 +116,9 @@
 
         remote(2, j).start()
         remote(3, j).start()
+
+    for j in range(WINDOW):
+        send(j)
 
     def gather(ref, c, count):
         parts = [ref.at[k][pl.ds(c, count, stride=cells), :] for k in range(2)]
@@ -161,56 +165,102 @@
         for c in range(cells):
             got = [crit.at[k][pl.ds(j * few * cells + c, few, stride=cells), :] for k in range(2)]
             s_ref[c, modes + j * few : modes + (j + 1) * few, :] = jnp.concatenate(got, axis=1)
+        for way in range(4):
+            remote(way, j).wait_send()
+        if j + WINDOW < CHUNKS:
+            send(j + WINDOW)
 
     total[...] = jnp.zeros_like(total)
     columns = s_ref.shape[1]
 
-    @pl.loop(0, cells // 4)
+    @pl.loop(0, cells // GROUP)
     def _(g):
-        pieces = [split3(s_ref[g * 4 + q]) for q in range(4)]
+        pieces = [split3(s_ref[g * GROUP + q]) for q in range(GROUP)]
         a, b, d = [jnp.concatenate(kind, axis=1) for kind in zip(*pieces)]
         total[0:columns] += dot_t(b, b)
         total[columns:] += dot_t(jnp.concatenate([a, b, d], axis=0), a)
 
     cross = total[2 * columns : 3 * columns] + total[3 * columns :]
     store_pieces(part, total[columns : 2 * columns] + (total[0:columns] + (cross + cross.T)))
-    for j in range(CHUNKS):
-        for way in range(4):
-            remote(way, j).wait_send()
     reduce_all(nx, nz, part, sum_ref, inbox, reduce_sems)
 
-
-def halo_call(velocity, scaled_modes, nx, nz):
+    factor(load_tiles(sum_ref, scale), upper_ref, inverse_ref)
+    wa, wb, wc = split3(inverse_ref[...])
+    main = jnp.concatenate(
+        [
+            jnp.concatenate([wa, wa], axis=1),
+            jnp.concatenate([wb, wb], axis=1),
+            jnp.concatenate([wc, jnp.zeros_like(wc)], axis=1),
+        ],
+        axis=0,
+    )
+    total[0 : 2 * columns] = jnp.zeros((2 * columns, columns), F32)
+
+    @pl.loop(0, cells // GROUP)
+    def _(g):
+        tops, lows = [], []
+        for q in range(GROUP):
+            sa, sb, sc = split3(s_ref[g * GROUP + q])
+            y = dot(main, jnp.concatenate([sa, sb], axis=0))
+            x = y[0:columns] + (y[columns : 2 * columns] + y[2 * columns :] + dot(wa, sc))
+            x_ref[g * GROUP + q] = x
+            a, b = split2(x)
+            tops.append(a)
+            lows.append(b)
+        a = jnp.concatenate(tops, axis=1)
+        both = jnp.concatenate([a, jnp.concatenate(lows, axis=1)], axis=0)
+        total[0 : 2 * columns] += dot_t(both, a)
+
+    store = pltpu.make_async_copy(x_ref, x_hbm, load_sem.at[CHUNKS + 2])
+    store.start()
+    cross = total[columns : 2 * columns]
+    store_pieces(part_two, total[0:columns] + (cross + cross.T))
+    reduce_all(nx, nz, part_two, sum_two_ref, inbox_two, reduce_two)
+    store.wait()
+
+
+def halo_call(velocity, scaled_modes, nx, nz, scale):
     snaps, _, cells_x, cells_z, width = velocity.shape
     modes = scaled_modes.shape[0]
     fields = snaps * 3
     cells = cells_x * cells_z
     columns = modes + snaps
+    pieces = jax.ShapeDtypeStruct((PIECES, columns // PIECES, columns), F32)
     x_face = pltpu.VMEM((fields, cells_z, width), F32)
     z_face = pltpu.VMEM((fields * cells_x, width), F32)
     return pl.pallas_call(
-        functools.partial(halo_kernel, nx, nz),
+        functools.partial(halo_kernel, nx, nz, scale),
         out_shape=(
             jax.ShapeDtypeStruct((cells, columns, width), F32),
-            jax.ShapeDtypeStruct((PIECES, columns // PIECES, columns), F32),
+            pieces,
+            jax.ShapeDtypeStruct((columns, columns), F32),
         ),
         in_specs=[pl.BlockSpec(memory_space=pl.ANY)] * 2,
-        out_specs=[pl.BlockSpec(memory_space=pltpu.VMEM)] * 2,
+        out_specs=[
+            pl.BlockSpec(memory_space=pl.ANY),
+            pl.BlockSpec(memory_space=pltpu.VMEM),
+            pl.BlockSpec(memory_space=pltpu.VMEM),
+        ],
         scratch_shapes=[
+            pltpu.VMEM((cells, columns, width), F32),
+            pltpu.VMEM((cells, columns, width), F32),
+            pltpu.VMEM((columns, columns), F32),
+            pltpu.VMEM(pieces.shape, F32),
             pltpu.VMEM((fields, cells_x, cells_z, width), F32),
             pltpu.VMEM((2, snaps * cells, width // 2), F32),
             pltpu.VMEM((2, modes * cells, width // 2), F32),
             x_face, x_face, z_face, z_face, z_face, z_face,
             pltpu.VMEM((4 * columns, columns), F32),
-            pltpu.SemaphoreType.DMA((CHUNKS + 2,)),
+            pltpu.SemaphoreType.DMA((CHUNKS + 3,)),
             pltpu.SemaphoreType.DMA((4, CHUNKS)),
             pltpu.SemaphoreType.DMA((4, CHUNKS)),
+            *reduce_scratch(nx * nz, columns),
             *reduce_scratch(nx * nz, columns),
         ],
         compiler_params=pltpu.CompilerParams(
             collective_id=0, has_side_effects=True, vmem_limit_bytes=VMEM_LIMIT
         ),
-        name="halo_criterion_gram",
+        name="halo_to_first_pass",
     )(velocity.reshape(fields, cells_x, cells_z, width), scaled_modes.reshape(modes * cells, width))
 
 
@@ -358,65 +408,48 @@
     ]
 
 
-def factor_one_kernel(scale, sum_ref, lower_ref, upper_ref, inverse_ref):
+def second_kernel(
+    scale, x_hbm, sum_ref, upper_one_ref, out_hbm, triangle_ref, lower_one_ref,
+    x_ref, buffer, inverse_ref, upper_ref, load_sem, store_sem,
+):
+    columns, _, width = out_hbm.shape
+    blocks = x_hbm.shape[0] // 8
+    half = width // 2
+
+    def load(i):
+        part = pl.ds(i * 8, 8)
+        return pltpu.make_async_copy(x_hbm.at[part], x_ref.at[part], load_sem.at[i])
+
+    def store(i, k):
+        where = out_hbm.at[:, pl.ds(i * 8, 8), pl.ds(k * half, half)]
+        return pltpu.make_async_copy(buffer.at[i, k], where, store_sem.at[i, k])
+
+    for i in range(blocks):
+        load(i).start()
     factor(load_tiles(sum_ref, scale), upper_ref, inverse_ref)
-    lower_ref[...] = upper_ref[...].T
-
-
-def first_kernel(nx, nz, s_ref, inverse_ref, x_ref, sum_ref, total, part, inbox, reduce_sems):
-    greet(nx, nz)
-    wa, wb, wc = split3(inverse_ref[...])
-    columns = wa.shape[0]
-    main = jnp.concatenate(
-        [
-            jnp.concatenate([wa, wa], axis=1),
-            jnp.concatenate([wb, wb], axis=1),
-            jnp.concatenate([wc, jnp.zeros_like(wc)], axis=1),
-        ],
-        axis=0,
-    )
-    total[...] = jnp.zeros_like(total)
-
-    @pl.loop(0, s_ref.shape[0] // 4)
-    def _(g):
-        high, low = [], []
-        for q in range(4):
-            sa, sb, sc = split3(s_ref[g * 4 + q])
-            y = dot(main, jnp.concatenate([sa, sb], axis=0))
-            x = y[0:columns] + (y[columns : 2 * columns] + y[2 * columns :] + dot(wa, sc))
-            x_ref[g * 4 + q] = x
-            a, b = split2(x)
-            high.append(a)
-            low.append(b)
-        a = jnp.concatenate(high, axis=1)
-        total[...] += dot_t(jnp.concatenate([a, jnp.concatenate(low, axis=1)], axis=0), a)
-
-    cross = total[columns:]
-    store_pieces(part, total[0:columns] + (cross + cross.T))
-    pl.semaphore_wait(pltpu.get_barrier_semaphore(), nx * nz - 1)
-    reduce_all(nx, nz, part, sum_ref, inbox, reduce_sems)
-
-
-def second_kernel(
-    scale, x_ref, sum_ref, upper_one_ref, out_ref, triangle_ref, inverse_ref, upper_ref
-):
-    @pl.when(pl.program_id(0) == 0)
-    def _():
-        factor(load_tiles(sum_ref, scale), upper_ref, inverse_ref)
-        triangle_ref[...] = lax.dot_general(
-            upper_ref[...], upper_one_ref[...], (((1,), (0,)), ((), ())),
-            precision=lax.Precision.HIGHEST, preferred_element_type=F32,
-        )
-
     wa, wb = split2(inverse_ref[...])
-    columns, _, width = out_ref.shape
     both = jnp.concatenate(
         [jnp.concatenate([wa, wa], axis=1), jnp.concatenate([wb, jnp.zeros_like(wb)], axis=1)],
         axis=0,
     )
-    for c in range(x_ref.shape[0]):
-        y = dot(both, jnp.concatenate(split2(x_ref[c]), axis=0))
-        out_ref[:, c, :] = y[0:columns] + y[columns:]
+    for i in range(blocks):
+        load(i).wait()
+        for c in range(8):
+            y = dot(both, jnp.concatenate(split2(x_ref[i * 8 + c]), axis=0))
+            q = y[0:columns] + y[columns:]
+            for k in range(2):
+                flat = buffer.at[i, k].reshape(columns * 8, half)
+                flat[pl.ds(c, columns, stride=8), :] = q[:, k * half : (k + 1) * half]
+        for k in range(2):
+            store(i, k).start()
+    lower_one_ref[...] = upper_one_ref[...].T
+    triangle_ref[...] = lax.dot_general(
+        upper_ref[...], upper_one_ref[...], (((1,), (0,)), ((), ())),
+        precision=lax.Precision.HIGHEST, preferred_element_type=F32,
+    )
+    for i in range(blocks):
+        for k in range(2):
+            store(i, k).wait()
 
 
 def shards(velocity, scaled_modes):
@@ -429,40 +462,21 @@
     whole = pl.BlockSpec(memory_space=pltpu.VMEM)
     params = pltpu.CompilerParams(vmem_limit_bytes=VMEM_LIMIT)
 
-    stacked, sum_one = halo_call(velocity, scaled_modes, nx, nz)
-    lower_one, upper_one, inverse_one = pl.pallas_call(
-        functools.partial(factor_one_kernel, scale),
-        out_shape=(square, square, square), in_specs=[whole], out_specs=[whole] * 3,
-        compiler_params=params, name="factor_one",
-    )(sum_one)
-    first_pass, sum_two = pl.pallas_call(
-        functools.partial(first_kernel, nx, nz),
-        out_shape=(
-            jax.ShapeDtypeStruct(stacked.shape, F32),
-            jax.ShapeDtypeStruct(sum_one.shape, F32),
-        ),
-        in_specs=[whole] * 2,
-        out_specs=[whole] * 2,
+    first_pass, sum_two, upper_one = halo_call(velocity, scaled_modes, nx, nz, scale)
+    blocks = cells // 8
+    basis, triangle, lower_one = pl.pallas_call(
+        functools.partial(second_kernel, scale),
+        out_shape=(jax.ShapeDtypeStruct((columns, cells, width), F32), square, square),
+        in_specs=[pl.BlockSpec(memory_space=pl.ANY), whole, whole],
+        out_specs=[pl.BlockSpec(memory_space=pl.ANY), whole, whole],
         scratch_shapes=[
-            pltpu.VMEM((2 * columns, columns), F32), *reduce_scratch(nx * nz, columns)
+            pltpu.VMEM((cells, columns, width), F32),
+            pltpu.VMEM((blocks, 2, columns, 8, width // 2), F32),
+            pltpu.VMEM((columns, columns), F32),
+            pltpu.VMEM((columns, columns), F32),
+            pltpu.SemaphoreType.DMA((blocks,)),
+            pltpu.SemaphoreType.DMA((blocks, 2)),
         ],
-        compiler_params=pltpu.CompilerParams(
-            collective_id=1, has_side_effects=True, vmem_limit_bytes=VMEM_LIMIT
-        ),
-        name="first_pass_gram",
-    )(stacked, inverse_one)
-    still = pl.BlockSpec((columns, columns), lambda i: (0, 0))
-    basis, triangle = pl.pallas_call(
-        functools.partial(second_kernel, scale),
-        grid=(cells_x,),
-        out_shape=(jax.ShapeDtypeStruct((columns, cells, width), F32), square),
-        in_specs=[
-            pl.BlockSpec((cells_z, columns, width), lambda i: (i, 0, 0)),
-            pl.BlockSpec(sum_two.shape, lambda i: (0, 0, 0)),
-            still,
-        ],
-        out_specs=[pl.BlockSpec((columns, cells_z, width), lambda i: (0, i, 0)), still],
-        scratch_shapes=[pltpu.VMEM((columns, columns), F32)] * 2,
         compiler_params=params, name="second_pass",
     )(first_pass, sum_two, upper_one)
     return (basis.reshape(columns, cells_x, cells_z, width), triangle, lower_one)

time: 96.2 us -> 86.5 us (0.90)
  Pallas kernels: 95.3 us -> 85.6 us
    pallas_call x4 -> x2, Pallas kernels: 95.3 us -> 85.6 us  [the longest x1 76.1 us: halo_call(): pl.pallas_call(functools.partial(halo_kernel, nx, nz, scale), out_shape=(...]
where the time goes in v3:
time: 86.5 us; the launch traced here: 86.3 us
  Pallas kernels  85.6 us (99%)
    pallas_call x1, Pallas kernels, halo_call(): pl.pallas_call(functools.partial(halo_kernel, nx, nz, scale), out_shape=(...  76.1 us
    pallas_call x1, Pallas kernels, shards(): pl.pallas_call(functools.partial(second_kernel, scale), out_shape=(jax.Sh...  9.45 us

profile of v3, /device:TPU:0, one launch (start us, length us, event | category | flops | bytes accessed | tf_op | source)
XLA Modules:
  0.0 86.3 jit_solution(13533830125603904756)
XLA Ops:
  0.6 76.1 %halo_to_first_pass.1 = (f32[32,128,256]{2,1,0:T(8,128)}, f32[32,4,128]{2,1,0:T(4,128)}, f32[128,128]{1,0:T(8,128)}) custom-call(f32[192,4,8,256]{3,2,1,0:T(8,128)} %bitcast.3, f32[2048,256]{1,0:T(8,128)} %bitcast.4), custom_call_target="tpu_custom_call" | custom-call | tf_op jit(solution)/shard_map/halo_to_first_pass/pallas_call | solution.py:231
  76.7 9.5 %second_pass.1 = (f32[128,32,256]{2,1,0:T(8,128)}, f32[128,128]{1,0:T(8,128)}, f32[128,128]{1,0:T(8,128)}) custom-call(f32[32,128,256]{2,1,0:T(8,128)} %get-tuple-element.9.x_hbm, f32[32,4,128]{2,1,0:T(4,128)} %get-tuple-element.10.sum_ref, f32[128,128]{1,0:T(8,128)} %get-tuple-element.11.upper_one_ref), custom_call_target="tpu_custom_call" | custom-call | tf_op jit(solution)/shard_map/second_pass/pallas_call | solution.py:467

commit v4 on v3

--- a/solution.py
+++ b/solution.py
@@ -59,7 +59,7 @@
 
 def halo_kernel(
     nx, nz, scale, vel_hbm, modes_hbm, x_hbm, sum_two_ref, upper_ref,
-    s_ref, x_ref, inverse_ref, sum_ref, vel, crit, modes_split, x_low, x_high, z_low, z_high, z_first, z_last, total,
+    s_ref, pair_ref, third_ref, x_ref, inverse_ref, sum_ref, vel, crit, modes_split, x_low, x_high, z_low, z_high, z_first, z_last, total,
     load_sem, send_sem, recv_sem, part, inbox, reduce_sems, part_two, inbox_two, reduce_two,
 ):
     gx = lax.axis_index("gx")
@@ -101,10 +101,8 @@
         load(j).start()
     for k in range(2):
         load_modes(k).start()
-    pl.semaphore_wait(pltpu.get_barrier_semaphore(), nx * nz - 1)
-    def send(j):
-        remote(0, j).start()
-        remote(1, j).start()
+
+    def pack(j):
         load(j).wait()
 
         @pl.loop(j * per // group, (j + 1) * per // group)
@@ -114,11 +112,17 @@
             z_first[rows, :] = jnp.concatenate([b[:, 0, :] for b in blocks], axis=0)
             z_last[rows, :] = jnp.concatenate([b[:, cells_z - 1, :] for b in blocks], axis=0)
 
-        remote(2, j).start()
-        remote(3, j).start()
-
+    def send(j):
+        for way in range(4):
+            remote(way, j).start()
+
+    for j in range(WINDOW):
+        pack(j)
+    pl.semaphore_wait(pltpu.get_barrier_semaphore(), nx * nz - 1)
     for j in range(WINDOW):
         send(j)
+    for j in range(WINDOW, CHUNKS):
+        pack(j)
 
     def gather(ref, c, count):
         parts = [ref.at[k][pl.ds(c, count, stride=cells), :] for k in range(2)]
@@ -176,6 +180,10 @@
     @pl.loop(0, cells // GROUP)
     def _(g):
         pieces = [split3(s_ref[g * GROUP + q]) for q in range(GROUP)]
+        for q, (a, b, d) in enumerate(pieces):
+            pair_ref[g * GROUP + q, 0:columns, :] = a
+            pair_ref[g * GROUP + q, columns:, :] = b
+            third_ref[g * GROUP + q] = d
         a, b, d = [jnp.concatenate(kind, axis=1) for kind in zip(*pieces)]
         total[0:columns] += dot_t(b, b)
         total[columns:] += dot_t(jnp.concatenate([a, b, d], axis=0), a)
@@ -200,9 +208,9 @@
     def _(g):
         tops, lows = [], []
         for q in range(GROUP):
-            sa, sb, sc = split3(s_ref[g * GROUP + q])
-            y = dot(main, jnp.concatenate([sa, sb], axis=0))
-            x = y[0:columns] + (y[columns : 2 * columns] + y[2 * columns :] + dot(wa, sc))
+            y = dot(main, pair_ref[g * GROUP + q])
+            last = dot(wa, third_ref[g * GROUP + q])
+            x = y[0:columns] + (y[columns : 2 * columns] + y[2 * columns :] + last)
             x_ref[g * GROUP + q] = x
             a, b = split2(x)
             tops.append(a)
@@ -243,6 +251,8 @@
         ],
         scratch_shapes=[
             pltpu.VMEM((cells, columns, width), F32),
+            pltpu.VMEM((cells, 2 * columns, width), BF16),
+            pltpu.VMEM((cells, columns, width), BF16),
             pltpu.VMEM((cells, columns, width), F32),
             pltpu.VMEM((columns, columns), F32),
             pltpu.VMEM(pieces.shape, F32),
@@ -359,6 +369,16 @@
     shape = (8, size)
     lane = lax.broadcasted_iota(jnp.int32, shape, 1)
     sub = lax.broadcasted_iota(jnp.int32, shape, 0)
+    marks = [lane == sub + 8 * t for t in range(len(tiles))]
+    found = jnp.zeros(shape, F32)
+    for mark, tile in zip(marks, tiles):
+        found = jnp.where(mark, tile, found)
+    diagonal = jnp.broadcast_to(jnp.sum(found, axis=0, keepdims=True), shape)
+    shrink = 1.0 / jnp.sqrt(diagonal)
+    grow = diagonal * shrink
+    for t, mark in enumerate(marks):
+        side = jnp.sum(jnp.where(mark, shrink, 0.0), axis=1, keepdims=True)
+        tiles[t] = tiles[t] * jnp.broadcast_to(side, shape) * shrink
     for home in range(len(tiles)):
         k = home * 8
         tile = tiles[home]
@@ -371,7 +391,10 @@
         upper = jnp.zeros(shape, F32)
         inverse = jnp.zeros(shape, F32)
         for i in range(8):
-            inv.append(1.0 / pivot[i][i])
+            if i % 2 == 0:
+                one, both, two = pivot[i][i], pivot[i][i + 1], pivot[i + 1][i + 1]
+                inv.append(1.0 / one)
+                inv.append(one * (1.0 / (one * two - both * both)))
             fixed = jnp.where(lane == k + i, 1.0, rows[i])
             scale = jnp.sqrt(inv[i])
             upper = jnp.where((sub == i) & (lane >= k + i), rows[i] * scale, upper)
@@ -382,8 +405,8 @@
                 for m in range(j, 8):
                     pivot[j][m] = pivot[j][m] - ratio * pivot[i][m]
             rows[i] = fixed
-        upper_ref[k : k + 8, :] = upper
-        inverse_ref[k : k + 8, :] = inverse
+        upper_ref[k : k + 8, :] = upper * grow
+        inverse_ref[k : k + 8, :] = inverse * shrink
         inside = (lane >= k) & (lane < k + 8)
         clear = [jnp.where(inside & (lane > k + i), 0.0, rows[i]) for i in range(8)]
         for t in range(home + 1, len(tiles)):

time: 86.5 us -> 86.5 us (level)
  no operation moved by 1% of the time
where the time goes in v4:
time: 86.5 us; the launch traced here: 86.3 us
  Pallas kernels  85.5 us (99%)
    pallas_call x1, Pallas kernels, halo_call(): pl.pallas_call(functools.partial(halo_kernel, nx, nz, scale), out_shape=(...  76.1 us
    pallas_call x1, Pallas kernels, shards(): pl.pallas_call(functools.partial(second_kernel, scale), out_shape=(jax.Sh...  9.38 us

profile of v4, /device:TPU:0, one launch (start us, length us, event | category | flops | bytes accessed | tf_op | source)
XLA Modules:
  0.0 86.3 jit_solution(17782756325957440330)
XLA Ops:
  0.6 76.1 %halo_to_first_pass.1 = (f32[32,128,256]{2,1,0:T(8,128)}, f32[32,4,128]{2,1,0:T(4,128)}, f32[128,128]{1,0:T(8,128)}) custom-call(f32[192,4,8,256]{3,2,1,0:T(8,128)} %bitcast.3, f32[2048,256]{1,0:T(8,128)} %bitcast.4), custom_call_target="tpu_custom_call" | custom-call | tf_op jit(solution)/shard_map/halo_to_first_pass/pallas_call | solution.py:239
  76.8 9.4 %second_pass.1 = (f32[128,32,256]{2,1,0:T(8,128)}, f32[128,128]{1,0:T(8,128)}, f32[128,128]{1,0:T(8,128)}) custom-call(f32[32,128,256]{2,1,0:T(8,128)} %get-tuple-element.9.x_hbm, f32[32,4,128]{2,1,0:T(4,128)} %get-tuple-element.10.sum_ref, f32[128,128]{1,0:T(8,128)} %get-tuple-element.11.upper_one_ref), custom_call_target="tpu_custom_call" | custom-call | tf_op jit(solution)/shard_map/second_pass/pallas_call | solution.py:490

commit v5 on v4

--- a/solution.py
+++ b/solution.py
@@ -11,8 +11,8 @@
 F32 = jnp.float32
 BF16 = jnp.bfloat16
 CHUNKS = 8
-WINDOW = 3
-GROUP = 8
+WINDOW = 8
+GROUP = 16
 PIECES = 32
 VMEM_LIMIT = 60 * 1024 * 1024
 

time: 86.5 us -> 85.8 us (level)
  no operation moved by 1% of the time
where the time goes in v5:
time: 85.8 us; the launch traced here: 85.7 us
  Pallas kernels  84.9 us (99%)
    pallas_call x1, Pallas kernels, halo_call(): pl.pallas_call(functools.partial(halo_kernel, nx, nz, scale), out_shape=(...  75.5 us
    pallas_call x1, Pallas kernels, shards(): pl.pallas_call(functools.partial(second_kernel, scale), out_shape=(jax.Sh...  9.38 us

profile of v5, /device:TPU:0, one launch (start us, length us, event | category | flops | bytes accessed | tf_op | source)
XLA Modules:
  0.0 85.7 jit_solution(16009359745557476304)
XLA Ops:
  0.6 75.5 %halo_to_first_pass.1 = (f32[32,128,256]{2,1,0:T(8,128)}, f32[32,4,128]{2,1,0:T(4,128)}, f32[128,128]{1,0:T(8,128)}) custom-call(f32[192,4,8,256]{3,2,1,0:T(8,128)} %bitcast.3, f32[2048,256]{1,0:T(8,128)} %bitcast.4), custom_call_target="tpu_custom_call" | custom-call | tf_op jit(solution)/shard_map/halo_to_first_pass/pallas_call | solution.py:239
  76.1 9.4 %second_pass.1 = (f32[128,32,256]{2,1,0:T(8,128)}, f32[128,128]{1,0:T(8,128)}, f32[128,128]{1,0:T(8,128)}) custom-call(f32[32,128,256]{2,1,0:T(8,128)} %get-tuple-element.9.x_hbm, f32[32,4,128]{2,1,0:T(4,128)} %get-tuple-element.10.sum_ref, f32[128,128]{1,0:T(8,128)} %get-tuple-element.11.upper_one_ref), custom_call_target="tpu_custom_call" | custom-call | tf_op jit(solution)/shard_map/second_pass/pallas_call | solution.py:490
